TPU v7x, 256 devices: a whole 4x4x8 slice. The times are simulated.
256 devices in a mesh: row: 8 (over z), col: 8 (over x, y_hi), layer: 4 (over y_lo, core).
Axes of the slice: x: 4, y: 4 (y_hi: 2, y_lo: 2; y = y_hi * 2 + y_lo), z: 8, core: 2. Of those that a mesh axis runs over, the one named last changes fastest.
Arguments:
- left_tiles: bfloat16 [8, 4, 8, 3, 256, 256], P('row', 'layer', 'col'), may hold values from 0.0099487305 to 1
- left_slots: int32 [8, 4, 8, 3], P('row', 'layer', 'col'), may hold values from 0 to 8, as said below
- right_tiles: bfloat16 [8, 4, 8, 6, 256, 256], P('row', 'layer', 'col'), may hold values from 0.01 to 10
- right_slots: int32 [8, 4, 8, 6], P('row', 'layer', 'col'), may hold values from 0 to 16, as said below
Outputs:
- inflated: float32 [4096, 8192], P(('row', 'layer'), 'col')
Inputs may be any that keep to these rules, and one draw needn't show every extreme that they name: `left_slots`: in each device's list the slots below 8 are distinct tile positions (tile row p // 4, tile column p % 4); the value 2 * 4 marks an unused entry and may stand anywhere in the list. Every tile row of every device's block has a listed tile, and some device uses all 3 entries. `right_slots`: in each device's list the slots below 16 are distinct tile positions (inner tile row p // 4, tile column p % 4); the value 4 * 4 marks an unused entry and may stand anywhere in the list. Every inner tile row of every device's block has a listed tile, and some device uses all 6 entries.
All inputs are finite; a program needn't handle non-finite values.
Results may differ from a plain program's by a relative error of at most 0.0003.
Values may be sent and summed in bfloat16 or wider, within the bound.
A program may use at most 192 MiB of HBM per device.

v0:
```python
import jax
import jax.numpy as jnp
from jax import lax
from jax.sharding import PartitionSpec as P

TILE = 256
ROW_DEV = 512
COL_DEV = 1024
INNER_T = 32


def densify(tile_list, targets, cells):
    onehot = (targets[:, None] == jnp.arange(cells, dtype=jnp.int32)[None, :]).astype(jnp.bfloat16)
    return jnp.einsum("sp,stu->ptu", onehot, tile_list, preferred_element_type=jnp.float32).astype(
        jnp.bfloat16
    )


def arrange(tile_grid, grid_rows, grid_cols):
    tile_edge = tile_grid.shape[-1]
    shaped = tile_grid.reshape(grid_rows, grid_cols, tile_edge, tile_edge)
    return shaped.transpose(0, 2, 1, 3).reshape(grid_rows * tile_edge, grid_cols * tile_edge)


def slab_columns(tile_block, slot_block, tile_rows, inner_tiles, capacity):
    tile_edge = tile_block.shape[-1]
    listed = slot_block.size
    tile_list = tile_block.reshape(listed, tile_edge, tile_edge)
    slot_list = slot_block.reshape(listed)
    sources = listed // capacity
    source = jnp.arange(listed, dtype=jnp.int32) // capacity
    unused = slot_list >= tile_rows * inner_tiles
    targets = (
        slot_list // inner_tiles * (inner_tiles * sources)
        + source * inner_tiles
        + slot_list % inner_tiles
    )
    targets = jnp.where(unused, -1, targets)
    return arrange(
        densify(tile_list, targets, tile_rows * inner_tiles * sources),
        tile_rows,
        inner_tiles * sources,
    )


def panel_rows(tile_block, slot_block, inner_tiles, col_tiles, capacity):
    tile_edge = tile_block.shape[-1]
    listed = slot_block.size
    tile_list = tile_block.reshape(listed, tile_edge, tile_edge)
    slot_list = slot_block.reshape(listed)
    sources = listed // capacity
    source = jnp.arange(listed, dtype=jnp.int32) // capacity
    unused = slot_list >= inner_tiles * col_tiles
    targets = jnp.where(unused, -1, source * (inner_tiles * col_tiles) + slot_list)
    return arrange(
        densify(tile_list, targets, inner_tiles * col_tiles * sources),
        inner_tiles * sources,
        col_tiles,
    )


def local(left_tiles, left_slots, right_tiles, right_slots):
    row_tiles = ROW_DEV // TILE
    col_tiles = COL_DEV // TILE
    left_inner = INNER_T // lax.axis_size("col")
    right_inner = INNER_T // lax.axis_size("row")
    left_cap = left_slots.shape[3]
    right_cap = right_slots.shape[3]
    right_panel = panel_rows(right_tiles, right_slots, right_inner, col_tiles, right_cap)
    whole_right = lax.all_gather(right_panel, "row", axis=0, tiled=True)
    left_panel = slab_columns(left_tiles, left_slots, row_tiles, left_inner, left_cap)
    whole_left = lax.all_gather(left_panel, "col", axis=1, tiled=True)
    own_rows = lax.psum_scatter(
        jnp.dot(whole_left, whole_right, preferred_element_type=jnp.float32),
        "layer",
        scatter_dimension=0,
        tiled=True,
    )
    squares = own_rows * own_rows
    totals = lax.psum(jnp.sum(squares, axis=1), "col")
    return COL_DEV * lax.axis_size("col") * squares / totals[:, None]


def solution(mesh):
    return jax.shard_map(
        local,
        mesh=mesh,
        in_specs=(
            P("row", "layer", "col", None, None, None),
            P("row", "layer", "col", None),
            P("row", "layer", "col", None, None, None),
            P("row", "layer", "col", None),
        ),
        out_specs=P(("row", "layer"), "col"),
        check_vma=False,
    )
```

profile of v0, /device:TPU:1, one launch (start us, length us, event | category | flops | bytes accessed | tf_op | source)
XLA Modules:
  0.0 376.5 jit_solution(7070924947612065310)
XLA Ops:
  6.5 0.0 copy-start
  6.5 0.0 all-gather.3.cloned.1.call-start
  6.5 0.7 compare_select_fusion.1
  7.3 0.0 copy-start.1
  7.3 1.6 convolution_convert_fusion.1
  8.9 0.3 reshape.118
  9.2 0.4 copy.8
  9.6 1.2 copy.11
  10.8 0.0 all-gather.3.cloned.1.call-update
  10.8 0.0 all-gather.5.cloned.1.call-start
  10.9 0.9 convolution_convert_fusion
  11.8 2.1 reshape.122
  13.9 2.3 copy.10
  16.2 1.9 copy.12
  18.1 0.0 all-gather.5.cloned.1.call-update
  18.1 0.0 reduce-scatter.2.cloned.1.call-start
  18.1 110.2 %all-gather.3.cloned.1.call-done = bf16[512,8192]{1,0:T(8,128)(2,1)} async-done(((bf16[512,1024]{1,0:T(8,128)(2,1)}), bf16[512,8192]{1,0:T(8,128)(2,1)}) %all-gather.3.cloned.1.call-update) | async-done | bytes 8388624 | tf_op jit(solution)/shard_map/all_gather | solution.py:72
  128.3 172.9 %all-gather.5.cloned.1.call-done = bf16[8192,1024]{1,0:T(8,128)(2,1)} async-done(((bf16[1024,1024]{1,0:T(8,128)(2,1)}), bf16[8192,1024]{1,0:T(8,128)(2,1)}) %all-gather.5.cloned.1.call-update) | async-done | bytes 16777232 | tf_op jit(solution)/shard_map/all_gather | solution.py:70
  301.2 15.8 %fusion.13 = f32[512,1024]{1,0:T(8,128)} fusion(bf16[512,8192]{1,0:T(8,128)(2,1)} %all-gather.3.cloned.1.call-done, bf16[8192,1024]{1,0:T(8,128)(2,1)} %all-gather.5.cloned.1.call-done), kind=kOutput, calls=%fused_computation.31 | convolution fusion | flops 8589934592 | bytes 27262976 | tf_op jit(solution)/shard_map/dot_general | solution.py:74
  317.0 0.0 reduce-scatter.2.cloned.1.call-update
  317.0 29.8 %reduce-scatter.2.cloned.1.call-done = f32[128,1024]{1,0:T(8,128)} async-done(((f32[512,1024]{1,0:T(8,128)}), f32[128,1024]{1,0:T(8,128)}) %reduce-scatter.2.cloned.1.call-update) | async-done | bytes 524304 | tf_op jit(solution)/shard_map/reduce_scatter | solution.py:73
  346.9 1.2 multiply_reduce_fusion
  348.0 20.0 %psum.7 = f32[128]{0:T(128)S(1)} all-reduce(f32[128]{0:T(128)S(1)} %multiply_reduce_fusion), channel_id=1, replica_groups=mesh['row'=8,'col'=8,'layer'=4] {'col'}, use_global_device_ids=true, to_apply=%region_2.3 | all-reduce | flops 128 | bytes 1024 | tf_op jit(solution)/shard_map/psum | solution.py:80
  368.1 1.9 multiply_divide_fusion
  (3 shorter events, 0.0 us)
Async XLA Ops:
  6.5 4.3 %copy-start = (bf16[1,1,1,6,256,256]{5,4,3,2,1,0:T(8,128)(2,1)S(1)}, bf16[1,1,1,6,256,256]{5,4,3,2,1,0:T(8,128)(2,1)}, u32[]{:S(2)}) copy-start(bf16[1,1,1,6,256,256]{5,4,3,2,1,0:T(8,128)(2,1)} %param.6) | copy-start | bytes 2359300
  6.5 121.8 %all-gather.3.cloned.1.call-start = ((), (), s32[]{:S(2)}) async-start(), calls=%async_computation.1 | async-start | bytes 9437184 | tf_op jit(solution)/shard_map/all_gather | solution.py:72
  7.3 3.6 copy-start.1
  10.8 290.4 %all-gather.5.cloned.1.call-start = ((), (), s32[]{:S(2)}) async-start(), calls=%async_computation.2 | async-start | bytes 18874368 | tf_op jit(solution)/shard_map/all_gather | solution.py:70
  18.1 328.8 %reduce-scatter.2.cloned.1.call-start = ((), (), s32[]{:S(2)}) async-start(), calls=%async_computation.3 | async-start | bytes 2621440 | tf_op jit(solution)/shard_map/reduce_scatter | solution.py:73
Sparse Core Ops, SparseCore 0:
  10.9 117.3 all-gather.2
  130.1 171.0 all-gather.4
  317.2 29.6 reduce-scatter.1
where the time goes:
time: 379 us; the launch traced here: 377 us
  waiting for transfers between devices  313 us (83%)
  blocking collectives  20 us (5%)
  matrix products  18.3 us (5%)
  between operations  13.2 us (3%)
  local copies, waits for them, and re-layouts  8.12 us (2%)
  other arithmetic  3.85 us (1%)
    all_gather x1, waiting for transfers between devices, local(): whole_right = lax.all_gather(right_panel, 'row', axis=0, tiled=True)  173 us
    all_gather x1, waiting for transfers between devices, local(): whole_left = lax.all_gather(left_panel, 'col', axis=1, tiled=True)  110 us
    reduce_scatter x1, waiting for transfers between devices, local(): lax.psum_scatter(jnp.dot(whole_left, whole_right, preferred_element_type=...  29.8 us
    psum x1, blocking collectives, local(): totals = lax.psum(jnp.sum(squares, axis=1), 'col')  20 us
    dot_general x1, matrix products, local(): jnp.dot(whole_left, whole_right, preferred_element_type=jnp.float32)  15.8 us
  transfers between devices with their start and end apart: 3, of which 3 were waited for; matrix products, arithmetic and copies ran while one was open for 2% of the time, Pallas kernels for 0%

commit v1 on v0

v1 whole, which is shorter than its diff:
```python
import jax
import jax.numpy as jnp
from jax import lax
from jax.experimental import pallas as pl
from jax.experimental.pallas import tpu as pltpu
from jax.sharding import PartitionSpec as P

MESH = pl.DeviceIdType.MESH
T = 256
H = 128
N = 8
CAP_A, CAP_B = 3, 6
KT = 4
COL_T = 4
ROW_T = 2
COLS = 8192
LANE_A = 64
HALF = CAP_B // 2
FROM_LEFT, FROM_RIGHT = (1, 2, 3), (1, 2, 3)


def kernel(
    lt, ls, rt, rs, out,
    own0, l10, l20, l30, r10, r20, r30, x40,
    own1, l11, l21, l31, r11, r21, r31, x41,
    abuf, adense, bdense, acc, in1, in2, lanes,
    mytab, ztab, ctab, zsm, csm, mytot, ctot,
    zs, zr, as_, ar, tzs, tzr, tcs, tcr, tos, tor, s1s, s1r, s2s, s2r, loc,
):
    row = lax.axis_index("row")
    col = lax.axis_index("col")
    layer = lax.axis_index("layer")
    core, ylo = layer % 2, layer // 2
    pending = []
    own, x4 = (own0, own1), (x40, x41)
    l1, l2, l3 = (l10, l11), (l20, l21), (l30, l31)
    r1, r2, r3 = (r10, r11), (r20, r21), (r30, r31)

    def send(src, dst, ss, rs_, device):
        copy = pltpu.make_async_remote_copy(
            src_ref=src, dst_ref=dst, send_sem=ss, recv_sem=rs_, device_id=device, device_id_type=MESH
        )
        copy.start()
        pending.append(copy)

    def received(dst, rs_, ss):
        pltpu.make_async_remote_copy(
            src_ref=dst, dst_ref=dst, send_sem=ss, recv_sem=rs_, device_id={"row": (row + 1) % N}, device_id_type=MESH
        ).wait_recv()

    core_peer = {"layer": ylo * 2 + (1 - core)}
    y_peer = {"layer": (1 - ylo) * 2 + core}
    peers = [{"row": (row + o) % N} for o in range(1, N)]
    peers += [{"col": (col + o) % N} for o in range(1, N)]
    peers += [core_peer, y_peer]
    barrier = pltpu.get_barrier_semaphore()
    for peer in peers:
        pl.semaphore_signal(barrier, inc=1, device_id=peer, device_id_type=MESH)

    local = [pltpu.make_async_copy(lt, abuf.at[col, pl.ds(0, CAP_A)], loc.at[0])]
    for h in range(2):
        local.append(
            pltpu.make_async_copy(rt.at[:, :, pl.ds(h * H, H)], own[h].at[pl.ds(0, CAP_B)], loc.at[1 + h])
        )
    for copy in local:
        copy.start()
    for h in range(2):
        for ref in (own, l1, l2, l3, r1, r2, r3, x4):
            ref[h][CAP_B] = jnp.zeros((T, H), jnp.bfloat16)
    for c in range(N):
        abuf[c, CAP_A] = jnp.zeros((T, T), jnp.bfloat16)

    lane = lax.broadcasted_iota(jnp.int32, (8, 128), 1)
    table = jnp.where(lane < LANE_A, CAP_B, CAP_A)
    for s in range(CAP_B):
        table = jnp.where(lane == rs[s], s, table)
    for s in range(CAP_A):
        table = jnp.where(lane == ls[s] + LANE_A, s, table)
    mytab[...] = table
    ztab[row] = table
    ctab[col] = table

    pl.semaphore_wait(barrier, len(peers))

    right, left = {"row": (row + 1) % N}, {"row": (row + N - 1) % N}
    xright, xleft = {"col": (col + 2) % N}, {"col": (col + N - 2) % N}
    ypair_col = col + 1 - 2 * (col % 2)
    ypair = {"col": ypair_col}

    from_left = [None, l1, l2, l3, x4]
    from_right = [None, r1, r2, r3, x4]

    def z_send_right(h, d, q):
        k = h * 7 + (d - 1) * 2 + q
        piece = pl.ds(q * HALF, HALF)
        src = rt.at[piece, :, pl.ds(h * H, H)] if d == 1 else from_left[d - 1][h].at[piece]
        send(src, from_left[d][h].at[piece], zs.at[0, k], zr.at[0, k], right)

    def z_send_left(h, d, q):
        k = h * 7 + (d - 1) * 2 + q
        piece = pl.ds((1 - q) * HALF, HALF)
        src = rt.at[piece, :, pl.ds(h * H, H)] if d == 1 else from_right[d - 1][h].at[piece]
        send(src, from_right[d][h].at[piece], zs.at[1, k], zr.at[1, k], left)

    def z_step(k):
        h, m = k // 7, k % 7
        d, q = m // 2 + 1, m % 2
        received(from_left[d][h].at[pl.ds(q * HALF, HALF)], zr.at[0, k], zs.at[0, k])
        if d < 3 or (d == 3 and q == 0):
            z_send_right(h, d + 1, q)
        received(from_right[d][h].at[pl.ds((1 - q) * HALF, HALF)], zr.at[1, k], zs.at[1, k])
        if d < 3 or (d == 3 and q == 0):
            z_send_left(h, d + 1, q)
        if h == 0 and m in (5, 6):
            z_send_right(1, 1, m - 5)
            z_send_left(1, 1, m - 5)

    def a_send(i, block, part, device):
        ref = abuf.at[block, pl.ds(0, CAP_A)] if part is None else abuf.at[block, pl.ds(0, CAP_A), pl.ds(part * H, H)]
        send(ref, ref, as_.at[i], ar.at[i], device)

    def a_received(i, block, part):
        ref = abuf.at[block, pl.ds(0, CAP_A)] if part is None else abuf.at[block, pl.ds(0, CAP_A), pl.ds(part * H, H)]
        received(ref, ar.at[i], as_.at[i])

    def a_first(base, block):
        a_send(base, block, None, xright)
        a_send(base + 1, block, None, xleft)

    def a_forward(base, block):
        a_received(base, (block + N - 2) % N, None)
        a_send(base + 2, (block + N - 2) % N, 0, xright)
        a_received(base + 1, (block + 2) % N, None)
        a_send(base + 3, (block + 2) % N, 1, xleft)

    def a_last(base, block):
        a_received(base + 2, (block + 4) % N, 0)
        a_received(base + 3, (block + 4) % N, 1)

    for q in range(2):
        z_send_right(0, 1, q)
        z_send_left(0, 1, q)
    local[0].wait()
    a_send(8, col, None, ypair)
    a_first(0, col)
    for o in range(1, N):
        send(mytab, ztab.at[row], tzs.at[o], tzr.at[o], {"row": (row + o) % N})
        send(mytab, ctab.at[col], tcs.at[o], tcr.at[o], {"col": (col + o) % N})
    acc[...] = jnp.zeros_like(acc)
    lanes[...] = jnp.zeros_like(lanes)
    local[1].wait()
    local[2].wait()

    def tables():
        for o in range(1, N):
            received(ztab.at[(row + N - o) % N], tzr.at[o], tzs.at[o])
            received(ctab.at[(col + N - o) % N], tcr.at[o], tcs.at[o])
        c1 = pltpu.make_async_copy(ztab, zsm, loc.at[3])
        c2 = pltpu.make_async_copy(ctab, csm, loc.at[4])
        c1.start()
        c2.start()
        c1.wait()
        c2.wait()

    def densify_a():
        def body(c, carry):
            for i in range(ROW_T):
                for kk in range(KT):
                    s = csm[c, 0, LANE_A + i * KT + kk]
                    adense[c, pl.ds(i * T, T), pl.ds(kk * T, T)] = abuf[c, s]
            return carry

        lax.fori_loop(0, N, body, 0)

    def compute(h, ref, j, after=None):
        for kk in range(KT):
            for jc in range(COL_T):
                s = zsm[j, 0, kk * COL_T + jc]
                bdense[jc // 2, pl.ds(kk * T, T), pl.ds((jc % 2) * H, H)] = ref[h][s]
        for n in range(2):
            for i in range(ROW_T):
                part = jnp.dot(
                    adense[j, pl.ds(i * T, T)], bdense[n], preferred_element_type=jnp.float32
                )
                acc[h, n, 0, i] += part[:H]
                acc[h, n, 1, i] += part[H:]
            if after is not None:
                after(h, n)

    def layer_send(h, n):
        send(acc.at[h, n, 1 - core], in1.at[h, n], s1s.at[h, n], s1r.at[h, n], core_peer)

    def layer_forward(h, n):
        received(in1.at[h, n], s1r.at[h, n], s1s.at[h, n])
        acc[h, n, core, 1 - ylo] += in1[h, n, 1 - ylo]
        send(acc.at[h, n, core, 1 - ylo], in2.at[h, n], s2s.at[h, n], s2r.at[h, n], y_peer)

    def layer_finish(h, n):
        received(in2.at[h, n], s2r.at[h, n], s2s.at[h, n])
        total = acc[h, n, core, ylo] + in1[h, n, ylo] + in2[h, n]
        squares = total * total
        for u in range(2):
            part = squares[:, u * H : (u + 1) * H]
            out[:, pl.ds((n * 2 + u) * T + h * H, H)] = part
            lanes[...] += part

    def at_left(d):
        return (row + N - d) % N

    def at_right(d):
        return (row + d) % N

    for k in range(14):
        z_step(k)
        if k == 2:
            a_forward(0, col)
        elif k == 3:
            tables()
        elif k == 4:
            a_received(8, ypair_col, None)
            a_first(4, ypair_col)
        elif k == 5:
            a_last(0, col)
        elif k == 6:
            a_forward(4, ypair_col)
        elif k == 8:
            a_last(4, ypair_col)
            densify_a()
            compute(0, own, row)
        elif k == 9:
            compute(0, l1, at_left(1))
            compute(0, r1, at_right(1))
            compute(0, l2, at_left(2))
            compute(0, r2, at_right(2))
        elif k == 10:
            compute(0, l3, at_left(3))
            compute(0, r3, at_right(3))
            compute(0, x4, at_left(4), layer_send)
        elif k == 11:
            layer_forward(0, 0)
            layer_forward(0, 1)
            compute(1, own, row)
            compute(1, l1, at_left(1))
            compute(1, r1, at_right(1))
        elif k == 12:
            layer_finish(0, 0)
            layer_finish(0, 1)
            compute(1, l2, at_left(2))
            compute(1, r2, at_right(2))
            compute(1, l3, at_left(3))
            compute(1, r3, at_right(3))
    compute(1, x4, at_left(4), layer_send)
    layer_forward(1, 0)
    layer_forward(1, 1)
    layer_finish(1, 0)
    layer_finish(1, 1)

    line = jnp.sum(lanes[...].T, axis=0, keepdims=True)
    line = jnp.broadcast_to(line, (8, 128))
    mytot[...] = line
    for o in range(1, N):
        send(mytot, ctot.at[col], tos.at[o], tor.at[o], {"col": (col + o) % N})
    ctot[col] = line
    for o in range(1, N):
        received(ctot.at[(col + N - o) % N], tor.at[o], tos.at[o])
    total = ctot[0]
    for c in range(1, N):
        total += ctot[c]
    scale = jnp.broadcast_to((COLS / total)[0:1], (H, H)).T
    for u in range(8):
        out[:, pl.ds(u * H, H)] *= scale
    for copy in pending:
        copy.wait_send()


def local(left_tiles, left_slots, right_tiles, right_slots):
    bf16, f32, i32 = jnp.bfloat16, jnp.float32, jnp.int32
    dma = pltpu.SemaphoreType.DMA
    block = pltpu.VMEM((CAP_B + 1, T, H), bf16)
    return pl.pallas_call(
        kernel,
        out_shape=jax.ShapeDtypeStruct((H, 1024), f32),
        in_specs=[
            pl.BlockSpec(memory_space=pltpu.VMEM),
            pl.BlockSpec(memory_space=pltpu.SMEM),
            pl.BlockSpec(memory_space=pltpu.VMEM),
            pl.BlockSpec(memory_space=pltpu.SMEM),
        ],
        out_specs=pl.BlockSpec(memory_space=pltpu.VMEM),
        scratch_shapes=[
            *[block] * 16,
            pltpu.VMEM((N, CAP_A + 1, T, T), bf16),
            pltpu.VMEM((N, ROW_T * T, KT * T), bf16),
            pltpu.VMEM((2, KT * T, T), bf16),
            pltpu.VMEM((2, 2, 2, 2, H, T), f32),
            pltpu.VMEM((2, 2, 2, H, T), f32),
            pltpu.VMEM((2, 2, H, T), f32),
            pltpu.VMEM((H, H), f32),
            pltpu.VMEM((8, 128), i32),
            pltpu.VMEM((N, 8, 128), i32),
            pltpu.VMEM((N, 8, 128), i32),
            pltpu.SMEM((N, 8, 128), i32),
            pltpu.SMEM((N, 8, 128), i32),
            pltpu.VMEM((8, 128), f32),
            pltpu.VMEM((N, 8, 128), f32),
            dma((2, 14)), dma((2, 14)),
            dma((9,)), dma((9,)),
            dma((N,)), dma((N,)), dma((N,)), dma((N,)), dma((N,)), dma((N,)),
            dma((2, 2)), dma((2, 2)), dma((2, 2)), dma((2, 2)),
            dma((5,)),
        ],
        compiler_params=pltpu.CompilerParams(
            collective_id=0, has_side_effects=True, vmem_limit_bytes=56 * 1024 * 1024
        ),
        cost_estimate=pl.CostEstimate(flops=8_600_000_000, bytes_accessed=2_000_000, transcendentals=0),
    )(
        left_tiles.reshape(CAP_A, T, T),
        left_slots.reshape(CAP_A),
        right_tiles.reshape(CAP_B, T, T),
        right_slots.reshape(CAP_B),
    )


def solution(mesh):
    return jax.shard_map(
        local,
        mesh=mesh,
        in_specs=(
            P("row", "layer", "col", None, None, None),
            P("row", "layer", "col", None),
            P("row", "layer", "col", None, None, None),
            P("row", "layer", "col", None),
        ),
        out_specs=P(("row", "layer"), "col"),
        check_vma=False,
    )
```

time: 379 us -> 92.2 us (0.24)
  waiting for transfers between devices: 313 us -> 0 us
  Pallas kernels: 0 us -> 90.2 us
  blocking collectives: 20 us -> 0 us
  matrix products: 18.3 us -> 0 us
  between operations: 13.2 us -> 0.01 us
  local copies, waits for them, and re-layouts: 8.12 us -> 1.89 us
  other arithmetic: 3.85 us -> 0 us
    all_gather x2 -> x0, waiting for transfers between devices: 283 us -> none  [the longest x1 173 us: local(): whole_right = lax.all_gather(right_panel, 'row', axis=0, tiled=True)]
    pallas_call x0 -> x1, Pallas kernels: none -> 90.2 us  [local(): pl.pallas_call(kernel, out_shape=jax.ShapeDtypeStruct((H, 1024), f32), in...]
    reduce_scatter x1 -> x0, waiting for transfers between devices: 29.8 us -> none  [local(): lax.psum_scatter(jnp.dot(whole_left, whole_right, preferred_element_type=...]
    psum x1 -> x0, blocking collectives: 20 us -> none  [local(): totals = lax.psum(jnp.sum(squares, axis=1), 'col')]
    dot_general x3 -> x0, matrix products: 18.3 us -> none  [the longest x1 15.8 us: local(): jnp.dot(whole_left, whole_right, preferred_element_type=jnp.float32)]
    reshape x4 -> x0, local copies, waits for them, and re-layouts: 5.04 us -> none  [arrange(): shaped = tile_grid.reshape(grid_rows, grid_cols, tile_edge, tile_edge)]
  transfers between devices with their start and end apart: 3 -> 0, of which waited for: 3 -> 0; matrix products, arithmetic and copies ran while one was open for 2% -> 0% of each run, Pallas kernels for 0% -> 0%
where the time goes in v1:
time: 92.2 us; the launch traced here: 92.1 us
  Pallas kernels  90.2 us (98%)
  local copies, waits for them, and re-layouts  1.89 us (2%)
    pallas_call x1, Pallas kernels, local(): pl.pallas_call(kernel, out_shape=jax.ShapeDtypeStruct((H, 1024), f32), in...  90.2 us
    unnamed x1, local copies, waits for them, and re-layouts  1.89 us

profile of v1, /device:TPU:1, one launch (start us, length us, event | category | flops | bytes accessed | tf_op | source)
XLA Modules:
  0.0 92.1 jit_solution(6637577898710366004)
XLA Ops:
  0.0 90.2 %shard_map.46 = f32[128,1024]{1,0:T(8,128)} custom-call(bf16[3,256,256]{2,1,0:T(8,128)(2,1)} %bitcast.5, s32[3]{0:T(128)} %bitcast.6, bf16[6,256,256]{2,1,0:T(8,128)(2,1)} %bitcast.4, s32[6]{0:T(128)} %bitcast.7), custom_call_target="tpu_custom_call" | custom-call | flops 8600000512 | bytes 2000000 | tf_op jit(solution)/shard_map/pallas_call | solution.py:280
  90.2 1.9 %copy.6 = f32[128,1024]{1,0:T(8,128)} copy(f32[128,1024]{1,0:T(8,128)} %shard_map.46) | data formatting | bytes 1048576

commit v2 on v1

--- a/solution.py
+++ b/solution.py
@@ -16,7 +16,6 @@
 COLS = 8192
 LANE_A = 64
 HALF = CAP_B // 2
-FROM_LEFT, FROM_RIGHT = (1, 2, 3), (1, 2, 3)
 
 
 def kernel(
@@ -24,7 +23,7 @@
     own0, l10, l20, l30, r10, r20, r30, x40,
     own1, l11, l21, l31, r11, r21, r31, x41,
     abuf, adense, bdense, acc, in1, in2, lanes,
-    mytab, ztab, ctab, zsm, csm, mytot, ctot,
+    ztab, ctab, zsm, csm, mytot, ctot,
     zs, zr, as_, ar, tzs, tzr, tcs, tcr, tos, tor, s1s, s1r, s2s, s2r, loc,
 ):
     row = lax.axis_index("row")
@@ -50,9 +49,11 @@
 
     core_peer = {"layer": ylo * 2 + (1 - core)}
     y_peer = {"layer": (1 - ylo) * 2 + core}
-    peers = [{"row": (row + o) % N} for o in range(1, N)]
-    peers += [{"col": (col + o) % N} for o in range(1, N)]
-    peers += [core_peer, y_peer]
+    right, left = {"row": (row + 1) % N}, {"row": (row + N - 1) % N}
+    xright, xleft = {"col": (col + 2) % N}, {"col": (col + N - 2) % N}
+    ypair_col = col + 1 - 2 * (col % 2)
+    ypair = {"col": ypair_col}
+    peers = [right, left, xright, xleft, ypair, core_peer, y_peer]
     barrier = pltpu.get_barrier_semaphore()
     for peer in peers:
         pl.semaphore_signal(barrier, inc=1, device_id=peer, device_id_type=MESH)
@@ -76,16 +77,10 @@
         table = jnp.where(lane == rs[s], s, table)
     for s in range(CAP_A):
         table = jnp.where(lane == ls[s] + LANE_A, s, table)
-    mytab[...] = table
     ztab[row] = table
     ctab[col] = table
 
     pl.semaphore_wait(barrier, len(peers))
-
-    right, left = {"row": (row + 1) % N}, {"row": (row + N - 1) % N}
-    xright, xleft = {"col": (col + 2) % N}, {"col": (col + N - 2) % N}
-    ypair_col = col + 1 - 2 * (col % 2)
-    ypair = {"col": ypair_col}
 
     from_left = [None, l1, l2, l3, x4]
     from_right = [None, r1, r2, r3, x4]
@@ -115,6 +110,22 @@
             z_send_right(1, 1, m - 5)
             z_send_left(1, 1, m - 5)
 
+    def z_table(d):
+        if d > 1:
+            received(ztab.at[(row + N - d + 1) % N], tzr.at[0, d - 1], tzs.at[0, d - 1])
+            received(ztab.at[(row + d - 1) % N], tzr.at[1, d - 1], tzs.at[1, d - 1])
+        lines = ztab.at[(row + N - d + 1) % N]
+        send(lines, lines, tzs.at[0, d], tzr.at[0, d], right)
+        if d < 4:
+            lines = ztab.at[(row + d - 1) % N]
+            send(lines, lines, tzs.at[1, d], tzr.at[1, d], left)
+
+    def a_table(i, block, device):
+        send(ctab.at[block], ctab.at[block], tcs.at[i], tcr.at[i], device)
+
+    def a_table_received(i, block):
+        received(ctab.at[block], tcr.at[i], tcs.at[i])
+
     def a_send(i, block, part, device):
         ref = abuf.at[block, pl.ds(0, CAP_A)] if part is None else abuf.at[block, pl.ds(0, CAP_A), pl.ds(part * H, H)]
         send(ref, ref, as_.at[i], ar.at[i], device)
@@ -126,35 +137,38 @@
     def a_first(base, block):
         a_send(base, block, None, xright)
         a_send(base + 1, block, None, xleft)
+        a_table(base, block, xright)
+        a_table(base + 1, block, xleft)
 
     def a_forward(base, block):
         a_received(base, (block + N - 2) % N, None)
         a_send(base + 2, (block + N - 2) % N, 0, xright)
+        a_table_received(base, (block + N - 2) % N)
+        a_table(base + 2, (block + N - 2) % N, xright)
         a_received(base + 1, (block + 2) % N, None)
         a_send(base + 3, (block + 2) % N, 1, xleft)
+        a_table_received(base + 1, (block + 2) % N)
 
     def a_last(base, block):
         a_received(base + 2, (block + 4) % N, 0)
         a_received(base + 3, (block + 4) % N, 1)
+        a_table_received(base + 2, (block + 4) % N)
 
     for q in range(2):
         z_send_right(0, 1, q)
         z_send_left(0, 1, q)
     local[0].wait()
     a_send(8, col, None, ypair)
+    a_table(8, col, ypair)
     a_first(0, col)
-    for o in range(1, N):
-        send(mytab, ztab.at[row], tzs.at[o], tzr.at[o], {"row": (row + o) % N})
-        send(mytab, ctab.at[col], tcs.at[o], tcr.at[o], {"col": (col + o) % N})
+    z_table(1)
     acc[...] = jnp.zeros_like(acc)
     lanes[...] = jnp.zeros_like(lanes)
     local[1].wait()
     local[2].wait()
 
     def tables():
-        for o in range(1, N):
-            received(ztab.at[(row + N - o) % N], tzr.at[o], tzs.at[o])
-            received(ctab.at[(col + N - o) % N], tcr.at[o], tcs.at[o])
+        received(ztab.at[(row + 4) % N], tzr.at[0, 4], tzs.at[0, 4])
         c1 = pltpu.make_async_copy(ztab, zsm, loc.at[3])
         c2 = pltpu.make_async_copy(ctab, csm, loc.at[4])
         c1.start()
@@ -212,12 +226,16 @@
 
     for k in range(14):
         z_step(k)
-        if k == 2:
+        if k == 0:
+            z_table(2)
+        elif k == 1:
+            z_table(3)
+        elif k == 2:
             a_forward(0, col)
-        elif k == 3:
-            tables()
+            z_table(4)
         elif k == 4:
             a_received(8, ypair_col, None)
+            a_table_received(8, ypair_col)
             a_first(4, ypair_col)
         elif k == 5:
             a_last(0, col)
@@ -225,6 +243,7 @@
             a_forward(4, ypair_col)
         elif k == 8:
             a_last(4, ypair_col)
+            tables()
             densify_a()
             compute(0, own, row)
         elif k == 9:
@@ -296,7 +315,6 @@
             pltpu.VMEM((2, 2, 2, H, T), f32),
             pltpu.VMEM((2, 2, H, T), f32),
             pltpu.VMEM((H, H), f32),
-            pltpu.VMEM((8, 128), i32),
             pltpu.VMEM((N, 8, 128), i32),
             pltpu.VMEM((N, 8, 128), i32),
             pltpu.SMEM((N, 8, 128), i32),
@@ -305,7 +323,7 @@
             pltpu.VMEM((N, 8, 128), f32),
             dma((2, 14)), dma((2, 14)),
             dma((9,)), dma((9,)),
-            dma((N,)), dma((N,)), dma((N,)), dma((N,)), dma((N,)), dma((N,)),
+            dma((2, 5)), dma((2, 5)), dma((9,)), dma((9,)), dma((N,)), dma((N,)),
             dma((2, 2)), dma((2, 2)), dma((2, 2)), dma((2, 2)),
             dma((5,)),
         ],

time: 92.2 us -> 90.9 us (0.986)
  Pallas kernels: 90.2 us -> 88.8 us
    pallas_call x1, Pallas kernels: 90.2 us -> 88.8 us  [local(): pl.pallas_call(kernel, out_shape=jax.ShapeDtypeStruct((H, 1024), f32), in...]
where the time goes in v2:
time: 90.9 us; the launch traced here: 90.7 us
  Pallas kernels  88.8 us (98%)
  local copies, waits for them, and re-layouts  1.89 us (2%)
    pallas_call x1, Pallas kernels, local(): pl.pallas_call(kernel, out_shape=jax.ShapeDtypeStruct((H, 1024), f32), in...  88.8 us
    unnamed x1, local copies, waits for them, and re-layouts  1.89 us

profile of v2, /device:TPU:1, one launch (start us, length us, event | category | flops | bytes accessed | tf_op | source)
XLA Modules:
  0.0 90.7 jit_solution(335846452709232897)
XLA Ops:
  0.0 88.8 %shard_map.46 = f32[128,1024]{1,0:T(8,128)} custom-call(bf16[3,256,256]{2,1,0:T(8,128)(2,1)} %bitcast.5, s32[3]{0:T(128)} %bitcast.6, bf16[6,256,256]{2,1,0:T(8,128)(2,1)} %bitcast.4, s32[6]{0:T(128)} %bitcast.7), custom_call_target="tpu_custom_call" | custom-call | flops 8600000512 | bytes 2000000 | tf_op jit(solution)/shard_map/pallas_call | solution.py:299
  88.8 1.9 %copy.6 = f32[128,1024]{1,0:T(8,128)} copy(f32[128,1024]{1,0:T(8,128)} %shard_map.46) | data formatting | bytes 1048576

commit v3 on v2

v3 whole, which is shorter than its diff:
```python
import jax
import jax.numpy as jnp
from jax import lax
from jax.experimental import pallas as pl
from jax.experimental.pallas import tpu as pltpu
from jax.sharding import PartitionSpec as P

MESH = pl.DeviceIdType.MESH
T = 256
H = 128
N = 8
CAP_A, CAP_B = 3, 6
KT = 4
COL_T = 4
Q = 64
ROW_T = 2
COLS = 8192
SENT_LATER = 24
LANE_A = 64
HALF = CAP_B // 2
ORDER = [(0, 1, 0), (0, 1, 1), (0, 2, 0), (0, 2, 1), (0, 3, 0), (0, 3, 1), (0, 4, 0)]
ORDER += [(1, 1, 0), (1, 1, 1), (2, 1, 0), (1, 2, 0), (1, 2, 1), (2, 1, 1), (1, 3, 0), (1, 3, 1)]
ORDER += [(2, 2, 0), (1, 4, 0), (2, 2, 1), (2, 3, 0), (2, 3, 1), (2, 4, 0)]


def kernel(
    lt, ls, rt, rs, out,
    own0, l10, l20, l30, r10, r20, r30, x40,
    own1, l11, l21, l31, r11, r21, r31, x41,
    own2, l12, l22, l32, r12, r22, r32, x42,
    raw,
    abuf, adense, bdense, bturned, acc, in1, in2, lanes,
    ztab, ctab, zsm, csm, mytot, ctot,
    zs, zr, as_, ar, tzs, tzr, tcs, tcr, tos, tor, s1s, s1r, s2s, s2r, loc,
):
    row = lax.axis_index("row")
    col = lax.axis_index("col")
    layer = lax.axis_index("layer")
    core, ylo = layer % 2, layer // 2
    pending = []
    own, x4 = (own0, own1, own2), (x40, x41, x42)
    l1, l2, l3 = (l10, l11, l12), (l20, l21, l22), (l30, l31, l32)
    r1, r2, r3 = (r10, r11, r12), (r20, r21, r22), (r30, r31, r32)

    def send(src, dst, ss, rs_, device):
        copy = pltpu.make_async_remote_copy(
            src_ref=src, dst_ref=dst, send_sem=ss, recv_sem=rs_, device_id=device, device_id_type=MESH
        )
        copy.start()
        pending.append(copy)

    def sent(count):
        for copy in pending[: max(count, 0)]:
            copy.wait_send()
        del pending[: max(count, 0)]

    def received(dst, rs_, ss):
        pltpu.make_async_remote_copy(
            src_ref=dst, dst_ref=dst, send_sem=ss, recv_sem=rs_, device_id={"row": (row + 1) % N}, device_id_type=MESH
        ).wait_recv()

    core_peer = {"layer": ylo * 2 + (1 - core)}
    y_peer = {"layer": (1 - ylo) * 2 + core}
    right, left = {"row": (row + 1) % N}, {"row": (row + N - 1) % N}
    xright, xleft = {"col": (col + 2) % N}, {"col": (col + N - 2) % N}
    ypair_col = col + 1 - 2 * (col % 2)
    ypair = {"col": ypair_col}
    peers = [right, left, xright, xleft, ypair, core_peer, y_peer]
    barrier = pltpu.get_barrier_semaphore()
    for peer in peers:
        pl.semaphore_signal(barrier, inc=1, device_id=peer, device_id_type=MESH)

    local = [pltpu.make_async_copy(lt, abuf.at[col, pl.ds(0, CAP_A)], loc.at[0])]
    local.append(pltpu.make_async_copy(rt.at[:, :, pl.ds(0, H)], own0.at[pl.ds(0, CAP_B)], loc.at[1]))
    local.append(pltpu.make_async_copy(rt.at[:, :, pl.ds(H, H)], raw, loc.at[2]))
    for copy in local:
        copy.start()
    pl.semaphore_wait(barrier, len(peers))

    from_left = [None, l1, l2, l3, x4]
    from_right = [None, r1, r2, r3, x4]

    def z_send(k):
        p, d, q = ORDER[k]
        for way, (held, device) in enumerate(((from_left, right), (from_right, left))):
            piece = pl.ds((q if way == 0 else 1 - q) * HALF, HALF)
            if d > 1:
                src = held[d - 1][p].at[piece]
            elif p == 0:
                src = rt.at[piece, :, pl.ds(0, H)]
            else:
                src = own[p].at[piece]
            send(src, held[d][p].at[piece], zs.at[way, k], zr.at[way, k], device)

    def z_step(k):
        p, d, q = ORDER[k]
        for way, held in enumerate((from_left, from_right)):
            piece = pl.ds((q if way == 0 else 1 - q) * HALF, HALF)
            received(held[d][p].at[piece], zr.at[way, k], zs.at[way, k])
        while len(started) < len(ORDER):
            j = len(started)
            p, d, q = ORDER[j]
            if j - k > (2 if p == 0 else 3) or (d > 1 and ORDER.index((p, d - 1, q)) > k):
                break
            started.append(j)
            z_send(j)

    def z_table(d):
        if d > 1:
            received(ztab.at[(row + N - d + 1) % N], tzr.at[0, d - 1], tzs.at[0, d - 1])
            received(ztab.at[(row + d - 1) % N], tzr.at[1, d - 1], tzs.at[1, d - 1])
        lines = ztab.at[(row + N - d + 1) % N]
        send(lines, lines, tzs.at[0, d], tzr.at[0, d], right)
        if d < 4:
            lines = ztab.at[(row + d - 1) % N]
            send(lines, lines, tzs.at[1, d], tzr.at[1, d], left)

    def a_table(i, block, device):
        send(ctab.at[block], ctab.at[block], tcs.at[i], tcr.at[i], device)

    def a_table_received(i, block):
        received(ctab.at[block], tcr.at[i], tcs.at[i])

    def a_send(i, block, part, device):
        ref = abuf.at[block, pl.ds(0, CAP_A)] if part is None else abuf.at[block, pl.ds(0, CAP_A), pl.ds(part * H, H)]
        send(ref, ref, as_.at[i], ar.at[i], device)

    def a_received(i, block, part):
        ref = abuf.at[block, pl.ds(0, CAP_A)] if part is None else abuf.at[block, pl.ds(0, CAP_A), pl.ds(part * H, H)]
        received(ref, ar.at[i], as_.at[i])

    def a_first(base, block):
        a_send(base, block, None, xright)
        a_send(base + 1, block, None, xleft)
        a_table(base, block, xright)
        a_table(base + 1, block, xleft)

    def a_forward(base, block):
        a_received(base, (block + N - 2) % N, None)
        a_send(base + 2, (block + N - 2) % N, 0, xright)
        a_table_received(base, (block + N - 2) % N)
        a_table(base + 2, (block + N - 2) % N, xright)
        a_received(base + 1, (block + 2) % N, None)
        a_send(base + 3, (block + 2) % N, 1, xleft)
        a_table_received(base + 1, (block + 2) % N)

    def a_last(base, block):
        a_received(base + 2, (block + 4) % N, 0)
        a_received(base + 3, (block + 4) % N, 1)
        a_table_received(base + 2, (block + 4) % N)

    started = [0, 1]
    z_send(0)
    z_send(1)
    for ref in (own, l1, l2, l3, r1, r2, r3, x4):
        ref[0][CAP_B] = jnp.zeros((T, H), jnp.bfloat16)
        for p in (1, 2):
            ref[p][CAP_B] = jnp.zeros((Q, T), jnp.bfloat16)
    for c in range(N):
        abuf[c, CAP_A] = jnp.zeros((T, T), jnp.bfloat16)

    low = lax.broadcasted_iota(jnp.int32, (H, H), 1) < Q
    lane = lax.broadcasted_iota(jnp.int32, (8, 128), 1)
    table = jnp.where(lane < LANE_A, CAP_B, CAP_A)
    for s in range(CAP_B):
        table = jnp.where(lane == rs[s], s, table)
    for s in range(CAP_A):
        table = jnp.where(lane == ls[s] + LANE_A, s, table)
    ztab[row] = table
    ctab[col] = table
    local[0].wait()
    a_send(8, col, None, ypair)
    a_table(8, col, ypair)
    a_first(0, col)
    z_table(1)
    acc[...] = jnp.zeros_like(acc)
    lanes[...] = jnp.zeros_like(lanes)
    local[1].wait()
    local[2].wait()
    for tile in range(CAP_B):
        turned = raw[tile].T
        own1[tile] = turned[:Q]
        own2[tile] = turned[Q:]

    def tables():
        received(ztab.at[(row + 4) % N], tzr.at[0, 4], tzs.at[0, 4])
        c1 = pltpu.make_async_copy(ztab, zsm, loc.at[3])
        c2 = pltpu.make_async_copy(ctab, csm, loc.at[4])
        c1.start()
        c2.start()
        c1.wait()
        c2.wait()

    def densify_a(first, last):
        def body(c, carry):
            for i in range(ROW_T):
                for kk in range(KT):
                    s = csm[c, 0, LANE_A + i * KT + kk]
                    adense[c, pl.ds(i * T, T), pl.ds(kk * T, T)] = abuf[c, s]
            return carry

        lax.fori_loop(first, last, body, 0)

    def compute(p, ref, j, after=None):
        for kk in range(KT):
            for jc in range(COL_T):
                s = zsm[j, 0, kk * COL_T + jc]
                if p == 0:
                    bdense[jc // 2, pl.ds(kk * T, T), pl.ds((jc % 2) * H, H)] = ref[p][s]
                else:
                    bturned[pl.ds(jc * Q, Q), pl.ds(kk * T, T)] = ref[p][s]
        for n in range(2) if p == 0 else (p + 1,):
            for i in range(ROW_T):
                rows = adense[j, pl.ds(i * T, T)]
                if p == 0:
                    part = jnp.dot(rows, bdense[n], preferred_element_type=jnp.float32)
                else:
                    part = lax.dot_general(
                        rows, bturned[...], (((1,), (1,)), ((), ())), preferred_element_type=jnp.float32
                    )
                acc[n, 0, i] += part[:H]
                acc[n, 1, i] += part[H:]
            if after is not None:
                after(n)

    def layer_send(n):
        send(acc.at[n, 1 - core], in1.at[n], s1s.at[n], s1r.at[n], core_peer)

    def layer_forward(n):
        received(in1.at[n], s1r.at[n], s1s.at[n])
        acc[n, core, 1 - ylo] += in1[n, 1 - ylo]
        send(acc.at[n, core, 1 - ylo], in2.at[n], s2s.at[n], s2r.at[n], y_peer)

    def layer_finish(n):
        received(in2.at[n], s2r.at[n], s2s.at[n])
        total = acc[n, core, ylo] + in1[n, ylo] + in2[n]
        squares = total * total
        lanes[...] += squares[:, :H] + squares[:, H:]
        for u in range(2):
            part = squares[:, u * H : (u + 1) * H]
            if n < 2:
                out[:, pl.ds((n * 2 + u) * T, H)] = part
                continue
            turned = pltpu.roll(part, Q, 1)
            for v in range(2):
                place = pl.ds((u * 2 + v) * T + H, H)
                if n == 2:
                    out[:, place] = turned if v else part
                else:
                    out[:, place] = jnp.where(low, out[:, place], part if v else turned)

    def at_left(d):
        return (row + N - d) % N

    def at_right(d):
        return (row + d) % N

    last = len(ORDER) - 1
    for k in range(last):
        z_step(k)
        if k >= 3:
            sent(len(pending) - SENT_LATER)
        if k == 0:
            z_table(2)
        elif k == 1:
            z_table(3)
        elif k == 2:
            z_table(4)
            a_forward(0, col)
            a_received(8, ypair_col, None)
            a_table_received(8, ypair_col)
            a_first(4, ypair_col)
        elif k == 4:
            a_last(0, col)
        elif k == 5:
            a_forward(4, ypair_col)
        elif k == 8:
            a_last(4, ypair_col)
            tables()
            densify_a(0, N // 2)
        elif k == 9:
            densify_a(N // 2, N)
        elif k == 10:
            compute(0, own, row)
            compute(0, l1, at_left(1))
        elif k == 11:
            compute(0, r1, at_right(1))
            compute(0, l2, at_left(2))
        elif k == 12:
            compute(0, r2, at_right(2))
            compute(0, l3, at_left(3))
        elif k == 13:
            compute(0, r3, at_right(3))
            compute(0, x4, at_left(4), layer_send)
        elif k == 14:
            compute(1, own, row)
            compute(1, l1, at_left(1))
            compute(1, r1, at_right(1))
            layer_forward(0)
            layer_forward(1)
        elif k == 15:
            compute(1, l2, at_left(2))
            compute(1, r2, at_right(2))
            compute(1, l3, at_left(3))
            compute(1, r3, at_right(3))
        elif k == 16:
            compute(1, x4, at_left(4), layer_send)
            compute(2, own, row)
            compute(2, l1, at_left(1))
            compute(2, r1, at_right(1))
        elif k == 17:
            layer_forward(2)
            layer_finish(0)
        elif k == 18:
            layer_finish(1)
            compute(2, l2, at_left(2))
            compute(2, r2, at_right(2))
        elif k == 19:
            compute(2, l3, at_left(3))
            compute(2, r3, at_right(3))
    z_step(last)
    compute(2, x4, at_left(4), layer_send)
    layer_finish(2)
    layer_forward(3)
    layer_finish(3)

    line = jnp.sum(lanes[...].T, axis=0, keepdims=True)
    line = jnp.broadcast_to(line, (8, 128))
    mytot[...] = line
    for o in range(1, N):
        send(mytot, ctot.at[col], tos.at[o], tor.at[o], {"col": (col + o) % N})
    ctot[col] = line
    sent(len(pending) - (N - 1))
    for o in range(1, N):
        received(ctot.at[(col + N - o) % N], tor.at[o], tos.at[o])
    total = ctot[0]
    for c in range(1, N):
        total += ctot[c]
    scale = jnp.broadcast_to((COLS / total)[0:1], (H, H)).T
    for u in range(8):
        out[:, pl.ds(u * H, H)] *= scale
    sent(len(pending))


def local(left_tiles, left_slots, right_tiles, right_slots):
    bf16, f32, i32 = jnp.bfloat16, jnp.float32, jnp.int32
    dma = pltpu.SemaphoreType.DMA
    block = pltpu.VMEM((CAP_B + 1, T, H), bf16)
    turned = pltpu.VMEM((CAP_B + 1, Q, T), bf16)
    return pl.pallas_call(
        kernel,
        out_shape=jax.ShapeDtypeStruct((H, 1024), f32),
        in_specs=[
            pl.BlockSpec(memory_space=pl.ANY),
            pl.BlockSpec(memory_space=pltpu.SMEM),
            pl.BlockSpec(memory_space=pl.ANY),
            pl.BlockSpec(memory_space=pltpu.SMEM),
        ],
        out_specs=pl.BlockSpec(memory_space=pltpu.VMEM),
        scratch_shapes=[
            *[block] * 8,
            *[turned] * 16,
            pltpu.VMEM((CAP_B, T, H), bf16),
            pltpu.VMEM((N, CAP_A + 1, T, T), bf16),
            pltpu.VMEM((N, ROW_T * T, KT * T), bf16),
            pltpu.VMEM((2, KT * T, T), bf16),
            pltpu.VMEM((4 * Q, KT * T), bf16),
            pltpu.VMEM((4, 2, 2, H, T), f32),
            pltpu.VMEM((4, 2, H, T), f32),
            pltpu.VMEM((4, H, T), f32),
            pltpu.VMEM((H, H), f32),
            pltpu.VMEM((N, 8, 128), i32),
            pltpu.VMEM((N, 8, 128), i32),
            pltpu.SMEM((N, 8, 128), i32),
            pltpu.SMEM((N, 8, 128), i32),
            pltpu.VMEM((8, 128), f32),
            pltpu.VMEM((N, 8, 128), f32),
            dma((2, len(ORDER))), dma((2, len(ORDER))),
            dma((9,)), dma((9,)),
            dma((2, 5)), dma((2, 5)), dma((9,)), dma((9,)), dma((N,)), dma((N,)),
            dma((4,)), dma((4,)), dma((4,)), dma((4,)),
            dma((5,)),
        ],
        compiler_params=pltpu.CompilerParams(
            collective_id=0, has_side_effects=True, vmem_limit_bytes=56 * 1024 * 1024
        ),
        cost_estimate=pl.CostEstimate(flops=8_600_000_000, bytes_accessed=2_000_000, transcendentals=0),
    )(
        left_tiles.reshape(CAP_A, T, T),
        left_slots.reshape(CAP_A),
        right_tiles.reshape(CAP_B, T, T),
        right_slots.reshape(CAP_B),
    )


def solution(mesh):
    return jax.shard_map(
        local,
        mesh=mesh,
        in_specs=(
            P("row", "layer", "col", None, None, None),
            P("row", "layer", "col", None),
            P("row", "layer", "col", None, None, None),
            P("row", "layer", "col", None),
        ),
        out_specs=P(("row", "layer"), "col"),
        check_vma=False,
    )
```

time: 90.9 us -> 87.1 us (0.958)
  Pallas kernels: 88.8 us -> 85.1 us
    pallas_call x1, Pallas kernels: 88.8 us -> 85.1 us  [local(): pl.pallas_call(kernel, out_shape=jax.ShapeDtypeStruct((H, 1024), f32), in...]
where the time goes in v3:
time: 87.1 us; the launch traced here: 87 us
  Pallas kernels  85.1 us (98%)
  local copies, waits for them, and re-layouts  1.89 us (2%)
    pallas_call x1, Pallas kernels, local(): pl.pallas_call(kernel, out_shape=jax.ShapeDtypeStruct((H, 1024), f32), in...  85.1 us
    unnamed x1, local copies, waits for them, and re-layouts  1.89 us

profile of v3, /device:TPU:1, one launch (start us, length us, event | category | flops | bytes accessed | tf_op | source)
XLA Modules:
  0.0 87.0 jit_solution(18114072262599192640)
XLA Ops:
  0.0 85.1 %shard_map.46 = f32[128,1024]{1,0:T(8,128)} custom-call(bf16[3,256,256]{2,1,0:T(8,128)(2,1)} %bitcast.5, s32[3]{0:T(128)} %bitcast.6, bf16[6,256,256]{2,1,0:T(8,128)(2,1)} %bitcast.4, s32[6]{0:T(128)} %bitcast.7), custom_call_target="tpu_custom_call" | custom-call | flops 8600000512 | bytes 2000000 | tf_op jit(solution)/shard_map/pallas_call | solution.py:350
  85.1 1.9 %copy.6 = f32[128,1024]{1,0:T(8,128)} copy(f32[128,1024]{1,0:T(8,128)} %shard_map.46) | data formatting | bytes 1048576

commit v4 on v3

--- a/solution.py
+++ b/solution.py
@@ -18,6 +18,7 @@
 SENT_LATER = 24
 LANE_A = 64
 HALF = CAP_B // 2
+LOWEST, STEPS, ZERO = -6.0, 65534 / 23, -32768
 ORDER = [(0, 1, 0), (0, 1, 1), (0, 2, 0), (0, 2, 1), (0, 3, 0), (0, 3, 1), (0, 4, 0)]
 ORDER += [(1, 1, 0), (1, 1, 1), (2, 1, 0), (1, 2, 0), (1, 2, 1), (2, 1, 1), (1, 3, 0), (1, 3, 1)]
 ORDER += [(2, 2, 0), (1, 4, 0), (2, 2, 1), (2, 3, 0), (2, 3, 1), (2, 4, 0)]
@@ -29,7 +30,7 @@
     own1, l11, l21, l31, r11, r21, r31, x41,
     own2, l12, l22, l32, r12, r22, r32, x42,
     raw,
-    abuf, adense, bdense, bturned, acc, in1, in2, lanes,
+    abuf, adense, bdense, bturned, acc, in1, in2, coded, incoded, lanes,
     ztab, ctab, zsm, csm, mytot, ctot,
     zs, zr, as_, ar, tzs, tzr, tcs, tcr, tos, tor, s1s, s1r, s2s, s2r, loc,
 ):
@@ -100,7 +101,7 @@
         while len(started) < len(ORDER):
             j = len(started)
             p, d, q = ORDER[j]
-            if j - k > (2 if p == 0 else 3) or (d > 1 and ORDER.index((p, d - 1, q)) > k):
+            if j - k > (2 if p == 0 else 4) or (d > 1 and ORDER.index((p, d - 1, q)) > k):
                 break
             started.append(j)
             z_send(j)
@@ -233,7 +234,9 @@
 
     def layer_finish(n):
         received(in2.at[n], s2r.at[n], s2s.at[n])
-        total = acc[n, core, ylo] + in1[n, ylo] + in2[n]
+        finish(n, acc[n, core, ylo] + in1[n, ylo] + in2[n])
+
+    def finish(n, total):
         squares = total * total
         lanes[...] += squares[:, :H] + squares[:, H:]
         for u in range(2):
@@ -248,6 +251,35 @@
                     out[:, place] = turned if v else part
                 else:
                     out[:, place] = jnp.where(low, out[:, place], part if v else turned)
+
+    def code(v):
+        steps = (jnp.log2(jnp.maximum(v, 2.0**LOWEST)) - LOWEST) * STEPS
+        steps = jnp.minimum(jnp.round(steps), 65534.0) - 32767.0
+        return jnp.where(v > 0, steps, float(ZERO)).astype(jnp.int32).astype(jnp.int16)
+
+    def decode(q):
+        steps = q.astype(jnp.int32).astype(jnp.float32)
+        v = jnp.exp2((steps + 32767.0) * (1.0 / STEPS) + LOWEST)
+        return jnp.where(steps > ZERO + 0.5, v, 0.0)
+
+    def across(c):
+        return {"layer": (1 - ylo) * 2 + c}
+
+    def last_send():
+        send(acc.at[3, 1 - core, ylo], in1.at[3, 0], s1s.at[3], s1r.at[3], core_peer)
+        for u in range(2):
+            c = core if u else 1 - core
+            coded[u] = code(acc[3, c, 1 - ylo])
+            send(coded.at[u], incoded.at[core], s2s.at[3 + u], s2r.at[3 + u], across(c))
+
+    def last_finish():
+        received(in1.at[3, 0], s1r.at[3], s1s.at[3])
+        total = acc[3, core, ylo] + in1[3, 0]
+        for u in range(2):
+            c = core if u else 1 - core
+            received(incoded.at[c], s2r.at[3 + u], s2s.at[3 + u])
+            total += decode(incoded[c])
+        finish(3, total)
 
     def at_left(d):
         return (row + N - d) % N
@@ -319,10 +351,10 @@
             compute(2, l3, at_left(3))
             compute(2, r3, at_right(3))
     z_step(last)
-    compute(2, x4, at_left(4), layer_send)
+    compute(2, x4, at_left(4))
+    last_send()
     layer_finish(2)
-    layer_forward(3)
-    layer_finish(3)
+    last_finish()
 
     line = jnp.sum(lanes[...].T, axis=0, keepdims=True)
     line = jnp.broadcast_to(line, (8, 128))
@@ -368,6 +400,8 @@
             pltpu.VMEM((4, 2, 2, H, T), f32),
             pltpu.VMEM((4, 2, H, T), f32),
             pltpu.VMEM((4, H, T), f32),
+            pltpu.VMEM((2, H, T), jnp.int16),
+            pltpu.VMEM((2, H, T), jnp.int16),
             pltpu.VMEM((H, H), f32),
             pltpu.VMEM((N, 8, 128), i32),
             pltpu.VMEM((N, 8, 128), i32),
@@ -378,7 +412,7 @@
             dma((2, len(ORDER))), dma((2, len(ORDER))),
             dma((9,)), dma((9,)),
             dma((2, 5)), dma((2, 5)), dma((9,)), dma((9,)), dma((N,)), dma((N,)),
-            dma((4,)), dma((4,)), dma((4,)), dma((4,)),
+            dma((4,)), dma((4,)), dma((5,)), dma((5,)),
             dma((5,)),
         ],
         compiler_params=pltpu.CompilerParams(

time: 87.1 us -> 85 us (0.976)
  Pallas kernels: 85.1 us -> 83 us
    pallas_call x1, Pallas kernels: 85.1 us -> 83 us  [local(): pl.pallas_call(kernel, out_shape=jax.ShapeDtypeStruct((H, 1024), f32), in...]
where the time goes in v4:
time: 85 us; the launch traced here: 84.9 us
  Pallas kernels  83 us (98%)
  local copies, waits for them, and re-layouts  1.89 us (2%)
    pallas_call x1, Pallas kernels, local(): pl.pallas_call(kernel, out_shape=jax.ShapeDtypeStruct((H, 1024), f32), in...  83 us
    unnamed x1, local copies, waits for them, and re-layouts  1.89 us

profile of v4, /device:TPU:1, one launch (start us, length us, event | category | flops | bytes accessed | tf_op | source)
XLA Modules:
  0.0 84.9 jit_solution(4653370902296194259)
XLA Ops:
  0.0 83.0 %shard_map.46 = f32[128,1024]{1,0:T(8,128)} custom-call(bf16[3,256,256]{2,1,0:T(8,128)(2,1)} %bitcast.5, s32[3]{0:T(128)} %bitcast.6, bf16[6,256,256]{2,1,0:T(8,128)(2,1)} %bitcast.4, s32[6]{0:T(128)} %bitcast.7), custom_call_target="tpu_custom_call" | custom-call | flops 8600000512 | bytes 2000000 | tf_op jit(solution)/shard_map/pallas_call | solution.py:382
  83.0 1.9 %copy.6 = f32[128,1024]{1,0:T(8,128)} copy(f32[128,1024]{1,0:T(8,128)} %shard_map.46) | data formatting | bytes 1048576

commit v5 on v4

--- a/solution.py
+++ b/solution.py
@@ -381,7 +381,7 @@
     turned = pltpu.VMEM((CAP_B + 1, Q, T), bf16)
     return pl.pallas_call(
         kernel,
-        out_shape=jax.ShapeDtypeStruct((H, 1024), f32),
+        out_shape=pltpu.VMEM((H, 1024), f32),
         in_specs=[
             pl.BlockSpec(memory_space=pl.ANY),
             pl.BlockSpec(memory_space=pltpu.SMEM),
@@ -416,7 +416,7 @@
             dma((5,)),
         ],
         compiler_params=pltpu.CompilerParams(
-            collective_id=0, has_side_effects=True, vmem_limit_bytes=56 * 1024 * 1024
+            collective_id=0, has_side_effects=True, vmem_limit_bytes=54 * 1024 * 1024
         ),
         cost_estimate=pl.CostEstimate(flops=8_600_000_000, bytes_accessed=2_000_000, transcendentals=0),
     )(

time: 85 us -> 83.1 us (0.978)
  local copies, waits for them, and re-layouts: 1.89 us -> 0.8 us
    unnamed x1, local copies, waits for them, and re-layouts: 1.89 us -> 0.8 us
where the time goes in v5:
time: 83.1 us; the launch traced here: 83 us
  Pallas kernels  82.2 us (99%)
    pallas_call x1, Pallas kernels, local(): pl.pallas_call(kernel, out_shape=pltpu.VMEM((H, 1024), f32), in_specs=[pl...  82.2 us

profile of v5, /device:TPU:1, one launch (start us, length us, event | category | flops | bytes accessed | tf_op | source)
XLA Modules:
  0.0 83.0 jit_solution(1314202286478188762)
XLA Ops:
  0.0 82.2 %shard_map.46 = f32[128,1024]{1,0:T(8,128)S(1)} custom-call(bf16[3,256,256]{2,1,0:T(8,128)(2,1)} %bitcast.5, s32[3]{0:T(128)} %bitcast.6, bf16[6,256,256]{2,1,0:T(8,128)(2,1)} %bitcast.4, s32[6]{0:T(128)} %bitcast.7), custom_call_target="tpu_custom_call" | custom-call | flops 8600000512 | bytes 2000000 | tf_op jit(solution)/shard_map/pallas_call | solution.py:382
  82.2 0.8 copy.6

commit v6 on v5

--- a/solution.py
+++ b/solution.py
@@ -15,6 +15,7 @@
 Q = 64
 ROW_T = 2
 COLS = 8192
+WAYS = (0, 1)
 SENT_LATER = 24
 LANE_A = 64
 HALF = CAP_B // 2
@@ -25,14 +26,14 @@
 
 
 def kernel(
-    lt, ls, rt, rs, out,
+    lt, left_slots, rt, right_slots, out,
     own0, l10, l20, l30, r10, r20, r30, x40,
     own1, l11, l21, l31, r11, r21, r31, x41,
     own2, l12, l22, l32, r12, r22, r32, x42,
     raw,
     abuf, adense, bdense, bturned, acc, in1, in2, coded, incoded, lanes,
     ztab, ctab, zsm, csm, mytot, ctot,
-    zs, zr, as_, ar, tzs, tzr, tcs, tcr, tos, tor, s1s, s1r, s2s, s2r, loc,
+    zs, zr, as_, ar, tzs, tzr, tcs, tcr, tos, tor, s1s, s1r, s2s, s2r, loc, ls, rs,
 ):
     row = lax.axis_index("row")
     col = lax.axis_index("col")
@@ -74,6 +75,8 @@
     local = [pltpu.make_async_copy(lt, abuf.at[col, pl.ds(0, CAP_A)], loc.at[0])]
     local.append(pltpu.make_async_copy(rt.at[:, :, pl.ds(0, H)], own0.at[pl.ds(0, CAP_B)], loc.at[1]))
     local.append(pltpu.make_async_copy(rt.at[:, :, pl.ds(H, H)], raw, loc.at[2]))
+    local.append(pltpu.make_async_copy(left_slots, ls, loc.at[5]))
+    local.append(pltpu.make_async_copy(right_slots, rs, loc.at[6]))
     for copy in local:
         copy.start()
     pl.semaphore_wait(barrier, len(peers))
@@ -81,30 +84,30 @@
     from_left = [None, l1, l2, l3, x4]
     from_right = [None, r1, r2, r3, x4]
 
-    def z_send(k):
+    def z_send(k, way):
+        held, device = ((from_left, right), (from_right, left))[way]
         p, d, q = ORDER[k]
-        for way, (held, device) in enumerate(((from_left, right), (from_right, left))):
+        piece = pl.ds((q if way == 0 else 1 - q) * HALF, HALF)
+        if d > 1:
+            src = held[d - 1][p].at[piece]
+        elif p == 0:
+            src = rt.at[piece, :, pl.ds(0, H)]
+        else:
+            src = own[p].at[piece]
+        send(src, held[d][p].at[piece], zs.at[way, k], zr.at[way, k], device)
+
+    def z_step(k):
+        for way in WAYS:
+            p, d, q = ORDER[k]
             piece = pl.ds((q if way == 0 else 1 - q) * HALF, HALF)
-            if d > 1:
-                src = held[d - 1][p].at[piece]
-            elif p == 0:
-                src = rt.at[piece, :, pl.ds(0, H)]
-            else:
-                src = own[p].at[piece]
-            send(src, held[d][p].at[piece], zs.at[way, k], zr.at[way, k], device)
-
-    def z_step(k):
-        p, d, q = ORDER[k]
-        for way, held in enumerate((from_left, from_right)):
-            piece = pl.ds((q if way == 0 else 1 - q) * HALF, HALF)
-            received(held[d][p].at[piece], zr.at[way, k], zs.at[way, k])
-        while len(started) < len(ORDER):
-            j = len(started)
-            p, d, q = ORDER[j]
-            if j - k > (2 if p == 0 else 4) or (d > 1 and ORDER.index((p, d - 1, q)) > k):
-                break
-            started.append(j)
-            z_send(j)
+            received((from_left, from_right)[way][d][p].at[piece], zr.at[way, k], zs.at[way, k])
+            while started[way] < len(ORDER):
+                j = started[way]
+                p, d, q = ORDER[j]
+                if j - k > (2 if p == 0 else 4) or (d > 1 and ORDER.index((p, d - 1, q)) > k):
+                    break
+                started[way] += 1
+                z_send(j, way)
 
     def z_table(d):
         if d > 1:
@@ -150,9 +153,10 @@
         a_received(base + 3, (block + 4) % N, 1)
         a_table_received(base + 2, (block + 4) % N)
 
-    started = [0, 1]
-    z_send(0)
-    z_send(1)
+    started = [2, 2]
+    for way in WAYS:
+        z_send(0, way)
+        z_send(1, way)
     for ref in (own, l1, l2, l3, r1, r2, r3, x4):
         ref[0][CAP_B] = jnp.zeros((T, H), jnp.bfloat16)
         for p in (1, 2):
@@ -163,6 +167,8 @@
     low = lax.broadcasted_iota(jnp.int32, (H, H), 1) < Q
     lane = lax.broadcasted_iota(jnp.int32, (8, 128), 1)
     table = jnp.where(lane < LANE_A, CAP_B, CAP_A)
+    local[3].wait()
+    local[4].wait()
     for s in range(CAP_B):
         table = jnp.where(lane == rs[s], s, table)
     for s in range(CAP_A):
@@ -384,9 +390,9 @@
         out_shape=pltpu.VMEM((H, 1024), f32),
         in_specs=[
             pl.BlockSpec(memory_space=pl.ANY),
-            pl.BlockSpec(memory_space=pltpu.SMEM),
             pl.BlockSpec(memory_space=pl.ANY),
-            pl.BlockSpec(memory_space=pltpu.SMEM),
+            pl.BlockSpec(memory_space=pl.ANY),
+            pl.BlockSpec(memory_space=pl.ANY),
         ],
         out_specs=pl.BlockSpec(memory_space=pltpu.VMEM),
         scratch_shapes=[
@@ -413,7 +419,9 @@
             dma((9,)), dma((9,)),
             dma((2, 5)), dma((2, 5)), dma((9,)), dma((9,)), dma((N,)), dma((N,)),
             dma((4,)), dma((4,)), dma((5,)), dma((5,)),
-            dma((5,)),
+            dma((7,)),
+            pltpu.SMEM((CAP_A,), i32),
+            pltpu.SMEM((CAP_B,), i32),
         ],
         compiler_params=pltpu.CompilerParams(
             collective_id=0, has_side_effects=True, vmem_limit_bytes=54 * 1024 * 1024

time: 83.1 us -> 82 us (0.987)
  Pallas kernels: 82.2 us -> 81.1 us
    pallas_call x1, Pallas kernels: 82.2 us -> 81.1 us  [local(): pl.pallas_call(kernel, out_shape=pltpu.VMEM((H, 1024), f32), in_specs=[pl...]
where the time goes in v6:
time: 82 us; the launch traced here: 81.9 us
  Pallas kernels  81.1 us (99%)
    pallas_call x1, Pallas kernels, local(): pl.pallas_call(kernel, out_shape=pltpu.VMEM((H, 1024), f32), in_specs=[pl...  81.1 us

profile of v6, /device:TPU:1, one launch (start us, length us, event | category | flops | bytes accessed | tf_op | source)
XLA Modules:
  0.0 81.9 jit_solution(16730591938303778342)
XLA Ops:
  0.0 81.1 %shard_map.46 = f32[128,1024]{1,0:T(8,128)S(1)} custom-call(bf16[3,256,256]{2,1,0:T(8,128)(2,1)} %bitcast.5, s32[3]{0:T(128)} %bitcast.6, bf16[6,256,256]{2,1,0:T(8,128)(2,1)} %bitcast.4, s32[6]{0:T(128)} %bitcast.7), custom_call_target="tpu_custom_call" | custom-call | flops 8600000512 | bytes 2000000 | tf_op jit(solution)/shard_map/pallas_call | solution.py:388
  81.1 0.8 copy.6

commit v7 on v6

--- a/solution.py
+++ b/solution.py
@@ -22,7 +22,7 @@
 LOWEST, STEPS, ZERO = -6.0, 65534 / 23, -32768
 ORDER = [(0, 1, 0), (0, 1, 1), (0, 2, 0), (0, 2, 1), (0, 3, 0), (0, 3, 1), (0, 4, 0)]
 ORDER += [(1, 1, 0), (1, 1, 1), (2, 1, 0), (1, 2, 0), (1, 2, 1), (2, 1, 1), (1, 3, 0), (1, 3, 1)]
-ORDER += [(2, 2, 0), (1, 4, 0), (2, 2, 1), (2, 3, 0), (2, 3, 1), (2, 4, 0)]
+ORDER += [(2, 2, 0), (2, 2, 1), (1, 4, 0), (2, 3, 0), (2, 3, 1), (2, 4, 0)]
 
 
 def kernel(
@@ -342,17 +342,17 @@
             compute(1, l3, at_left(3))
             compute(1, r3, at_right(3))
         elif k == 16:
-            compute(1, x4, at_left(4), layer_send)
             compute(2, own, row)
             compute(2, l1, at_left(1))
             compute(2, r1, at_right(1))
+            compute(2, l2, at_left(2))
+            compute(2, r2, at_right(2))
         elif k == 17:
-            layer_forward(2)
+            compute(1, x4, at_left(4), layer_send)
             layer_finish(0)
         elif k == 18:
+            layer_forward(2)
             layer_finish(1)
-            compute(2, l2, at_left(2))
-            compute(2, r2, at_right(2))
         elif k == 19:
             compute(2, l3, at_left(3))
             compute(2, r3, at_right(3))

time: 82 us -> 81.7 us (level)
  no operation moved by 1% of the time
where the time goes in v7:
time: 81.7 us
  Pallas kernels  80.9 us (99%)
    pallas_call x1, Pallas kernels, local(): pl.pallas_call(kernel, out_shape=pltpu.VMEM((H, 1024), f32), in_specs=[pl...  80.9 us

profile of v7, /device:TPU:1, one launch (start us, length us, event | category | flops | bytes accessed | tf_op | source)
XLA Modules:
  0.0 81.7 jit_solution(11052127150432794306)
XLA Ops:
  0.0 80.9 %shard_map.46 = f32[128,1024]{1,0:T(8,128)S(1)} custom-call(bf16[3,256,256]{2,1,0:T(8,128)(2,1)} %bitcast.5, s32[3]{0:T(128)} %bitcast.6, bf16[6,256,256]{2,1,0:T(8,128)(2,1)} %bitcast.4, s32[6]{0:T(128)} %bitcast.7), custom_call_target="tpu_custom_call" | custom-call | flops 8600000512 | bytes 2000000 | tf_op jit(solution)/shard_map/pallas_call | solution.py:388
  80.9 0.8 copy.6

commit v8 on v7

--- a/solution.py
+++ b/solution.py
@@ -271,12 +271,25 @@
     def across(c):
         return {"layer": (1 - ylo) * 2 + c}
 
-    def last_send():
-        send(acc.at[3, 1 - core, ylo], in1.at[3, 0], s1s.at[3], s1r.at[3], core_peer)
+    def last_rows(j, i):
+        rows = adense[j, pl.ds(pl.multiple_of(i * T, T), T)]
+        part = lax.dot_general(
+            rows, bturned[...], (((1,), (1,)), ((), ())), preferred_element_type=jnp.float32
+        )
+        acc[3, 0, i] += part[:H]
+        acc[3, 1, i] += part[H:]
+
+    def last_compute(j):
+        for kk in range(KT):
+            for jc in range(COL_T):
+                bturned[pl.ds(jc * Q, Q), pl.ds(kk * T, T)] = x4[2][zsm[j, 0, kk * COL_T + jc]]
+        last_rows(j, 1 - ylo)
         for u in range(2):
             c = core if u else 1 - core
             coded[u] = code(acc[3, c, 1 - ylo])
             send(coded.at[u], incoded.at[core], s2s.at[3 + u], s2r.at[3 + u], across(c))
+        last_rows(j, ylo)
+        send(acc.at[3, 1 - core, ylo], in1.at[3, 0], s1s.at[3], s1r.at[3], core_peer)
 
     def last_finish():
         received(in1.at[3, 0], s1r.at[3], s1s.at[3])
@@ -357,8 +370,7 @@
             compute(2, l3, at_left(3))
             compute(2, r3, at_right(3))
     z_step(last)
-    compute(2, x4, at_left(4))
-    last_send()
+    last_compute(at_left(4))
     layer_finish(2)
     last_finish()
 

time: 81.7 us -> 81.7 us (level)
  no operation moved by 1% of the time
where the time goes in v8:
time: 81.7 us; the launch traced here: 81.6 us
  Pallas kernels  80.8 us (99%)
    pallas_call x1, Pallas kernels, local(): pl.pallas_call(kernel, out_shape=pltpu.VMEM((H, 1024), f32), in_specs=[pl...  80.8 us

profile of v8, /device:TPU:1, one launch (start us, length us, event | category | flops | bytes accessed | tf_op | source)
XLA Modules:
  0.0 81.6 jit_solution(1841947952400313038)
XLA Ops:
  0.0 80.8 %shard_map.46 = f32[128,1024]{1,0:T(8,128)S(1)} custom-call(bf16[3,256,256]{2,1,0:T(8,128)(2,1)} %bitcast.5, s32[3]{0:T(128)} %bitcast.6, bf16[6,256,256]{2,1,0:T(8,128)(2,1)} %bitcast.4, s32[6]{0:T(128)} %bitcast.7), custom_call_target="tpu_custom_call" | custom-call | flops 8600000512 | bytes 2000000 | tf_op jit(solution)/shard_map/pallas_call | solution.py:400
  80.8 0.8 copy.6
